TPU v7x, 32 devices: a whole 2x2x4 slice. The times are simulated.
32 devices in a mesh: pair: 8 (over y, x, core), lam: 4 (over z).
Axes of the slice: x: 2, y: 2, z: 4, core: 2. Of those that a mesh axis runs over, the one named last changes fastest.
Arguments:
- integrals: bfloat16 [8, 32, 4, 64, 1024], P('pair', 'lam'), may hold values from -0.119628906 to 0.119628906
- tile_pair: int32 [8, 32], P('pair', 'lam'), may hold values from 0 to 15, as said below
- tile_lam: int32 [8, 32], P('pair', 'lam'), may hold values from 0 to 15, as said below
- tile_count: int32 [8, 4], P('pair', 'lam'), may hold values from 1 to 8, as said below
- mu_index: int32 [512], P('pair'), may hold values from 0 to 1023
- nu_index: int32 [512], P('pair'), may hold values from 0 to 1023
- occupied_coef: bfloat16 [1024, 16], replicated, may hold values from -1.5 to 1.5
- virtual_coef: bfloat16 [1024, 1280], replicated, may hold values from -1.5 to 1.5
Outputs:
- orbital_integrals: float32 [16, 1280, 20480], P('lam', 'pair')
Inputs may be any that keep to these rules, and one draw needn't show every extreme that they name: On every device the live and dead slots name distinct pairs of (tile_pair, tile_lam); tile_pair lies in 0 to 15. On lam index l every slot's tile_lam lies in l * 4 to (l + 1) * 4 - 1. Slots from tile_count on are dead and their integrals are ignored; some device has all 8 slots live.
All inputs are finite; a program needn't handle non-finite values.
Results may differ from a plain program's by a relative error of at most 0.0049.
Values may be sent and summed in bfloat16 or wider, within the bound.
A program may use at most 128 MiB of HBM per device.

v0:
```python
import math

import jax
import jax.numpy as jnp
from jax import lax
from jax.sharding import PartitionSpec as P


def tile_pass(partial_value, tile_group, occ_columns):
    tile_data, pair_list, lam_list, live_total = tile_group
    tile_rows = tile_data.shape[1]
    tile_depth = tile_data.shape[2]

    def add_tile(slot_index, running):
        row_start = pair_list[slot_index] * tile_rows
        occ_rows = lax.dynamic_slice_in_dim(
            occ_columns, lam_list[slot_index] * tile_depth, tile_depth, 0
        )
        contrib = jnp.einsum(
            "rls,lj->jrs", tile_data[slot_index], occ_rows, preferred_element_type=jnp.float32
        )
        current = lax.dynamic_slice_in_dim(running, row_start, tile_rows, 1)
        return lax.dynamic_update_slice_in_dim(running, current + contrib, row_start, 1)

    return lax.fori_loop(0, live_total, add_tile, partial_value)


def on_device(
    integrals, tile_pair, tile_lam, tile_count, mu_index, nu_index, occupied_coef, virtual_coef
):
    lam_count = lax.axis_size("lam")
    pair_count = lax.axis_size("pair")
    occ_total = occupied_coef.shape[1]
    vir_total = virtual_coef.shape[1]
    basis_count = occupied_coef.shape[0]
    rows_here = mu_index.shape[0]
    tile_data = integrals[0]
    pair_list = tile_pair[0]
    lam_list = tile_lam[0]
    live_total = tile_count[0, 0]
    tile_groups = (tile_data, pair_list, lam_list, live_total)
    occ_share = occ_total // lam_count
    partial_value = jnp.zeros((occupied_coef.shape[1], rows_here, basis_count), jnp.float32)
    partial_value = tile_pass(partial_value, tile_groups, occupied_coef)
    summed = lax.psum(partial_value, "lam")
    own_half = lax.dynamic_slice_in_dim(summed, lax.axis_index("lam") * occ_share, occ_share, 0)
    vir_share = vir_total // pair_count
    half_low = own_half.astype(jnp.bfloat16).reshape(occ_share * rows_here, basis_count)
    mixed = jnp.dot(half_low, virtual_coef, preferred_element_type=jnp.float32)
    mixed = mixed.astype(jnp.bfloat16).reshape(occ_share, rows_here, pair_count, vir_share)
    first_all, second_all = (
        lax.all_gather(mu_index, "pair", axis=0, tiled=True),
        lax.all_gather(nu_index, "pair", axis=0, tiled=True),
    )
    received = lax.all_to_all(mixed, "pair", split_axis=2, concat_axis=1, tiled=True)
    item_count = received.shape[0]
    total_rows = received.shape[1]
    column_count = received.shape[3]
    mixed_rows = received.reshape(item_count, total_rows, column_count)
    row_block = math.gcd(total_rows, 256)

    def add_rows(running, row_start):
        occ_rows = jnp.take(
            occupied_coef, lax.dynamic_slice_in_dim(first_all, row_start, row_block), axis=0
        ).astype(jnp.float32)
        vir_rows = jnp.take(
            virtual_coef, lax.dynamic_slice_in_dim(second_all, row_start, row_block), axis=0
        ).astype(jnp.float32)
        weights = (
            (occ_rows[:, :, None] * vir_rows[:, None, :])
            .astype(jnp.bfloat16)
            .reshape(row_block, occ_total * vir_total)
        )
        mixed_piece = lax.dynamic_slice_in_dim(mixed_rows, row_start, row_block, 1)
        return (
            running
            + jnp.einsum("qrb,rk->qbk", mixed_piece, weights, preferred_element_type=jnp.float32),
            None,
        )

    start_total = jnp.zeros((item_count, column_count, occ_total * vir_total), jnp.float32)
    result, _ = lax.scan(
        add_rows, start_total, jnp.arange(0, total_rows, row_block, dtype=jnp.int32)
    )
    return result


def solution(mesh):
    placed = (
        P("pair", "lam", None, None, None),
        P("pair", "lam"),
        P("pair", "lam"),
        P("pair", "lam"),
        P("pair"),
        P("pair"),
        P(),
        P(),
    )
    return jax.shard_map(
        on_device, mesh=mesh, in_specs=placed, out_specs=P("lam", "pair", None), check_vma=False
    )
```

profile of v0, /device:TPU:0, one launch (start us, length us, event | category | flops | bytes accessed | tf_op | source)
XLA Modules:
  0.0 354.7 jit_solution(16553714189256822451)
XLA Ops:
  0.0 2.5 broadcast_in_dim.33.clone
  2.5 40.1 %while.21 = (s32[]{:T(128)}, f32[16,64,1024]{2,1,0:T(8,128)}, s32[]{:T(128)}, s32[8]{0:T(128)S(1)}, s32[8]{0:T(128)S(1)}, /*index=5*/bf16[1024,16]{0,1:T(8,128)(...) while((s32[]{:T(128)}, f32[16,64,1024]{2,1,0:T(8,128)}, ...), condition=%wide.region_1.0_spmd, body=%wide.region_0.0_spmd.sunk | while | flops 8454157 | bytes 2101555 | solution.py:25
  5.8 1.1 constant_dynamic-slice_fusion.2
  6.9 1.4 convolution_add_fusion.2
  12.3 1.1 constant_dynamic-slice_fusion.2
  13.5 1.4 convolution_add_fusion.2
  18.9 1.1 constant_dynamic-slice_fusion.2
  20.0 1.4 convolution_add_fusion.2
  25.5 1.1 constant_dynamic-slice_fusion.2
  26.6 1.4 convolution_add_fusion.2
  32.1 1.1 constant_dynamic-slice_fusion.2
  33.2 1.4 convolution_add_fusion.2
  38.6 1.1 constant_dynamic-slice_fusion.2
  39.8 1.4 convolution_add_fusion.2
  42.7 158.4 %all-reduce.4 = bf16[16,64,1024]{2,1,0:T(8,128)(2,1)} all-reduce(f32[16,64,1024]{2,1,0:T(8,128)} %get-tuple-element.85), channel_id=1, replica_groups=mesh['pair'=8,'lam'=4] {'lam'}, use_global_device_ids=true, to_apply=%region_2.0 | all-reduce | flops 1048576 | bytes 6291456 | tf_op jit(solution)/shard_map/psum | solution.py:45
  203.0 2.3 reshape.62
  205.3 2.4 copy.15
  207.7 4.2 %all-to-all-start = ((bf16[4,64,8,160]{3,1,0,2:T(8,128)(2,1)}), bf16[4,64,8,160]{3,1,0,2:T(8,128)(2,1)}, u32[]{:S(2)}, u32[]{:S(2)}) async-start(bf16[4,64,8,160]{3,1,0,2:T(8,128)(2,1)} %copy.15), calls=%async_computation | async-start | bytes 2097152 | tf_op jit(solution)/shard_map/all_to_all | solution.py:55
  214.7 14.9 %all-reduce.2 = (s32[512]{0:T(512)S(1)}, s32[512]{0:T(512)S(1)}) all-reduce(s32[512]{0:T(512)S(1)} %dynamic-update-slice, s32[512]{0:T(512)S(1)} %dynamic-update-slice.1), channel_id=1, replica_groups=mesh['pair'=8,'lam'=4] {'pair'}, use_global_device_ids=true, to_apply=%add | all-reduce | flops 1024 | bytes 8192
  229.6 2.6 copy.16
  232.2 2.8 reshape.63
  234.9 119.8 %while.22 = (s32[]{:T(128)}, f32[4,160,20480]{2,1,0:T(8,128)}, s32[2]{0:T(128)S(1)}, bf16[4,512,160]{1,2,0:T(8,128)(2,1)}, s32[512]{0:T(512)S(1)}, /*index=5*/bf...) while((s32[]{:T(128)}, f32[4,160,20480]{2,1,0:T(8,128)}, ...), condition=%wide.region_4.5_spmd.clone, body=%wide.region_3.4_spmd.clone.sunk | while | flops 6748255232 | bytes 154412368 | solution.py:82
  239.1 1.2 gather_fusion
  240.4 1.2 select_convert_fusion.4
  241.6 6.7 %multiply_convert_fusion.2 = bf16[256,16,1280]{2,1,0:T(8,128)(2,1)} fusion(f32[256,1280]{1,0:T(8,128)} %select_convert_fusion.4, f32[256,16]{1,0:T(8,128)} %select_convert_fusion.5), kind=kLoop, calls=%fused_computation.11.clone.1 | loop fusion | flops 10485760 | bytes 11812864 | tf_op jit(solution)/shard_map/while/body/eval_jaxpr/convert_element_type | solution.py:71
  248.3 14.9 %reshape.108 = bf16[256,20480,1]{1,0,2:T(8,128)(2,1)} reshape(bf16[256,16,1280]{2,1,0:T(8,128)(2,1)} %multiply_convert_fusion.2) | data formatting | bytes 20971520 | tf_op jit(solution)/shard_map/while/body/eval_jaxpr/convert_element_type | solution.py:71
  263.2 23.1 %select_add_fusion.2 = f32[4,160,20480]{2,1,0:T(8,128)} fusion(f32[4,160,20480]{2,1,0:T(8,128)} %get-tuple-element.331, bf16[256,20480,1]{1,0,2:T(8,128)(2,1)} %reshape.108, pred[]{:T(512)S(6)} %compare.3, bf16[4,512,160]{1,2,0:T(8,128)(2,1)S(1)} %copy-done.1, s32[]{:T(128)S(6)} %select_n.68), kind=kOutput, calls=%fused_computation.10.clone.1 | convolution fusion | flops 6737100800 | bytes 115671048 | tf_op jit(solution)/shard_map/while/body/eval_jaxpr/qrb,rk->qbk/dot_general | solution.py:77
  290.5 1.2 gather_fusion
  291.7 1.2 select_convert_fusion.4
  293.0 6.7 %multiply_convert_fusion.2 = bf16[256,16,1280]{2,1,0:T(8,128)(2,1)} fusion(f32[256,1280]{1,0:T(8,128)} %select_convert_fusion.4, f32[256,16]{1,0:T(8,128)} %select_convert_fusion.5), kind=kLoop, calls=%fused_computation.11.clone.1 | loop fusion | flops 10485760 | bytes 11812864 | tf_op jit(solution)/shard_map/while/body/eval_jaxpr/convert_element_type | solution.py:71
  299.7 14.9 %reshape.108 = bf16[256,20480,1]{1,0,2:T(8,128)(2,1)} reshape(bf16[256,16,1280]{2,1,0:T(8,128)(2,1)} %multiply_convert_fusion.2) | data formatting | bytes 20971520 | tf_op jit(solution)/shard_map/while/body/eval_jaxpr/convert_element_type | solution.py:71
  314.5 40.1 %select_add_fusion.2 = f32[4,160,20480]{2,1,0:T(8,128)} fusion(f32[4,160,20480]{2,1,0:T(8,128)} %get-tuple-element.331, bf16[256,20480,1]{1,0,2:T(8,128)(2,1)} %reshape.108, pred[]{:T(512)S(6)} %compare.3, bf16[4,512,160]{1,2,0:T(8,128)(2,1)S(1)} %copy-done.1, s32[]{:T(128)S(6)} %select_n.68), kind=kOutput, calls=%fused_computation.10.clone.1 | convolution fusion | flops 6737100800 | bytes 115671048 | tf_op jit(solution)/shard_map/while/body/eval_jaxpr/qrb,rk->qbk/dot_general | solution.py:77
  (65 shorter events, 21.6 us)
Async XLA Ops:
  0.0 2.5 copy-start.3
  0.0 2.5 copy-start.2
  42.7 159.5 %copy-start = (bf16[1024,1280]{1,0:T(8,128)(2,1)S(1)}, bf16[1024,1280]{1,0:T(8,128)(2,1)}, u32[]{:S(2)}) copy-start(bf16[1024,1280]{1,0:T(8,128)(2,1)} %param.19) | copy-start | bytes 7864324
  202.1 10.8 %copy-start.6 = (u32[32]{0:T(128)S(1)}, u32[32]{0:T(128)}, u32[]{:S(2)}) copy-start(u32[32]{0:T(128)} %constant.71) | copy-start | bytes 388
  202.2 12.0 %copy-start.4 = (s32[64]{0:T(128)S(1)}, s32[64]{0:T(128)}, u32[]{:S(2)}) copy-start(s32[64]{0:T(128)} %param.16) | copy-start | bytes 772
  202.2 12.3 %copy-start.5 = (s32[64]{0:T(128)S(1)}, s32[64]{0:T(128)}, u32[]{:S(2)}) copy-start(s32[64]{0:T(128)} %param.17) | copy-start | bytes 772
  207.7 21.8 %all-to-all-start = ((bf16[4,64,8,160]{3,1,0,2:T(8,128)(2,1)}), bf16[4,64,8,160]{3,1,0,2:T(8,128)(2,1)}, u32[]{:S(2)}, u32[]{:S(2)}) async-start(bf16[4,64,8,160]{3,1,0,2:T(8,128)(2,1)} %copy.15), calls=%async_computation | async-start | bytes 2097152 | tf_op jit(solution)/shard_map/all_to_all | solution.py:55
  234.9 2.6 copy-start.7
  248.3 14.9 %copy-start.1 = (bf16[4,512,160]{1,2,0:T(8,128)(2,1)S(1)}, bf16[4,512,160]{1,2,0:T(8,128)(2,1)}, u32[]{:S(2)}) copy-start(bf16[4,512,160]{1,2,0:T(8,128)(2,1)} %get-tuple-element.344) | copy-start | bytes 1966084 | tf_op jit(solution)/shard_map/while
  263.2 23.1 %copy-start.8 = (s32[2]{0:T(128)S(1)}, s32[2]{0:T(128)}, u32[]{:S(2)}) copy-start(s32[2]{0:T(128)} %copy-done.7) | copy-start | bytes 28 | tf_op jit(solution)/shard_map/while
  286.3 2.6 copy-start.7
  299.7 14.9 %copy-start.1 = (bf16[4,512,160]{1,2,0:T(8,128)(2,1)S(1)}, bf16[4,512,160]{1,2,0:T(8,128)(2,1)}, u32[]{:S(2)}) copy-start(bf16[4,512,160]{1,2,0:T(8,128)(2,1)} %get-tuple-element.344) | copy-start | bytes 1966084 | tf_op jit(solution)/shard_map/while
  314.5 40.1 %copy-start.8 = (s32[2]{0:T(128)S(1)}, s32[2]{0:T(128)}, u32[]{:S(2)}) copy-start(s32[2]{0:T(128)} %copy-done.7) | copy-start | bytes 28 | tf_op jit(solution)/shard_map/while
where the time goes:
time: 354 us; the launch traced here: 355 us
  blocking collectives  173 us (49%)
  matrix products  72.2 us (20%)
  local copies, waits for them, and re-layouts  70.5 us (20%)
  other arithmetic  17.5 us (5%)
  loops' own time  16.2 us (5%)
  starting transfers between devices  4.24 us (1%)
    psum x1, blocking collectives, on_device(): summed = lax.psum(partial_value, 'lam')  158 us
    dot_general x2, matrix products, add_rows(): jnp.einsum('qrb,rk->qbk', mixed_piece, weights, preferred_element_type=jn...  63.2 us
    convert_element_type x2, local copies, waits for them, and re-layouts, add_rows(): weights = (occ_rows[:, :, None] * vir_rows[:, None, :]).astype(jnp.bfloat...  29.7 us
    unnamed x1, blocking collectives  14.9 us
    convert_element_type x2, other arithmetic, add_rows(): weights = (occ_rows[:, :, None] * vir_rows[:, None, :]).astype(jnp.bfloat...  13.4 us
    another operation x1, loops' own time, tile_pass(): return lax.fori_loop(0, live_total, add_tile, partial_value)  12.4 us
    dot_general x6, matrix products, add_tile(): jnp.einsum('rls,lj->jrs', tile_data[slot_index], occ_rows, preferred_elem...  8.19 us
  transfers between devices with their start and end apart: 1, of which 0 were waited for; matrix products, arithmetic and copies ran while one was open for 1% of the time, Pallas kernels for 0%

commit v1 on v0

v1 whole, which is shorter than its diff:
```python
import functools

import jax
import jax.numpy as jnp
from jax import lax
from jax.experimental import pallas as pl
from jax.experimental.pallas import tpu as pltpu
from jax.sharding import PartitionSpec as P

LANES = 128
ROW_TILE = 16
VMEM_BYTES = 50 * 1024 * 1024
MESH = pl.DeviceIdType.MESH


def round_up(value, step):
    return (value + step - 1) // step * step


def exchange_kernel(
    lam_n, pair_n, chunks, share, share_pad, rows,
    tiles_ref, spread_ref, place_ref, index_ref, occ_ref, vir_ref,
    lhs_ref, occ_rows_ref, vir_rows_ref,
    tile_buf, vir_buf, half_send, half_held, place_held, index_held, pick, mixed_t, mix_send, mix_held,
    tile_sem, vir_sem, place_ssem, place_rsem, index_ssem, index_rsem,
    half_ssem, half_rsem, mix_ssem, mix_rsem,
):
    lam_me = lax.axis_index("lam")
    pair_me = lax.axis_index("pair")
    groups = tile_buf.shape[0]
    depth = tile_buf.shape[1]
    basis = vir_buf.shape[0]

    barrier = pltpu.get_barrier_semaphore()
    for d in range(1, lam_n):
        pl.semaphore_signal(barrier, inc=1, device_id={"lam": lax.rem(lam_me + d, lam_n)}, device_id_type=MESH)
    for d in range(1, pair_n):
        pl.semaphore_signal(barrier, inc=1, device_id={"pair": lax.rem(pair_me + d, pair_n)}, device_id_type=MESH)

    tile_copies = [
        pltpu.make_async_copy(tiles_ref.at[pl.ds(q * depth, depth)], tile_buf.at[q], tile_sem.at[q])
        for q in range(groups)
    ]
    vir_copy = pltpu.make_async_copy(vir_ref, vir_buf, vir_sem)
    for copy in tile_copies:
        copy.start()
    vir_copy.start()

    for q in range(groups):
        tile_copies[q].wait()
        part = jnp.dot(spread_ref[q], tile_buf[q], preferred_element_type=jnp.float32).astype(jnp.bfloat16)
        for g in range(lam_n * chunks):
            half_send[g // chunks, g % chunks, q * ROW_TILE:(q + 1) * ROW_TILE, :] = part[
                g * ROW_TILE:(g + 1) * ROW_TILE
            ]

    pl.semaphore_wait(barrier, lam_n + pair_n - 2)

    sends = []
    place_copies, index_copies, half_copies, mix_copies = [], [], [], []
    for d in range(1, lam_n):
        peer = lax.rem(lam_me + d, lam_n)
        copy = pltpu.make_async_remote_copy(
            src_ref=place_ref, dst_ref=place_held.at[lam_me],
            send_sem=place_ssem.at[d], recv_sem=place_rsem.at[d],
            device_id={"lam": peer}, device_id_type=MESH,
        )
        copy.start()
        place_copies.append(copy)
    for d in range(1, pair_n):
        peer = lax.rem(pair_me + d, pair_n)
        copy = pltpu.make_async_remote_copy(
            src_ref=index_ref, dst_ref=index_held.at[pair_me],
            send_sem=index_ssem.at[d], recv_sem=index_rsem.at[d],
            device_id={"pair": peer}, device_id_type=MESH,
        )
        copy.start()
        index_copies.append(copy)
    for c in range(chunks):
        row_copies = []
        for d in range(1, lam_n):
            peer = lax.rem(lam_me + d, lam_n)
            copy = pltpu.make_async_remote_copy(
                src_ref=half_send.at[peer, c], dst_ref=half_held.at[c, lam_me],
                send_sem=half_ssem.at[c, d], recv_sem=half_rsem.at[c, d],
                device_id={"lam": peer}, device_id_type=MESH,
            )
            copy.start()
            row_copies.append(copy)
        half_copies.append(row_copies)

    place_held[lam_me] = place_ref[...]
    index_held[pair_me] = index_ref[...]
    for c in range(chunks):
        half_held[c, lam_me] = half_send[lam_me, c]

    for copy in index_copies:
        copy.wait_recv()
    for p in range(pair_n):
        line = index_held[p, 0:1, :].astype(jnp.float32)
        column = jnp.transpose(jnp.broadcast_to(line, (LANES, LANES)))
        for b in range(basis // LANES):
            name = (lax.broadcasted_iota(jnp.int32, (LANES, LANES), 1) + b * LANES).astype(jnp.float32)
            hit = jnp.where(column == name, 1.0, 0.0).astype(jnp.bfloat16)
            pick[0, p * rows:(p + 1) * rows, b * LANES:(b + 1) * LANES] = hit[:rows]
            pick[1, p * rows:(p + 1) * rows, b * LANES:(b + 1) * LANES] = hit[rows:]
    occ_rows_ref[...] = jnp.dot(pick[0], occ_ref[...], preferred_element_type=jnp.float32).astype(jnp.bfloat16)
    vir_copy.wait()
    step = 2 * LANES
    for n in range(0, vir_buf.shape[1], step):
        vir_rows_ref[:, n:n + step] = jnp.dot(
            pick[1], vir_buf[:, n:n + step], preferred_element_type=jnp.float32
        ).astype(jnp.bfloat16)

    for copy in place_copies:
        copy.wait_recv()
    place = jnp.transpose(place_held[...].reshape(-1, LANES).astype(jnp.float32)).astype(jnp.bfloat16)

    for c in range(chunks):
        for copy in half_copies[c]:
            copy.wait_recv()
        slots = half_held[c].reshape(-1, basis)
        half_low = jnp.dot(place, slots, preferred_element_type=jnp.float32).astype(jnp.bfloat16)
        for n in range(0, vir_buf.shape[1], step):
            mixed = jnp.dot(half_low, vir_buf[:, n:n + step], preferred_element_type=jnp.float32)
            mixed_t[n:n + step, :] = jnp.transpose(mixed)
        for p in range(pair_n):
            block = mixed_t[p * share:(p + 1) * share, :]
            if share_pad > share:
                block = jnp.concatenate([block, jnp.zeros((share_pad - share, LANES), jnp.float32)], axis=0)
            mix_send[c, p] = block.astype(jnp.bfloat16)
        row_copies = []
        for d in range(1, pair_n):
            peer = lax.rem(pair_me + d, pair_n)
            copy = pltpu.make_async_remote_copy(
                src_ref=mix_send.at[c, peer], dst_ref=mix_held.at[c, pair_me],
                send_sem=mix_ssem.at[c, d], recv_sem=mix_rsem.at[c, d],
                device_id={"pair": peer}, device_id_type=MESH,
            )
            copy.start()
            row_copies.append(copy)
        mix_copies.append(row_copies)
        mix_held[c, pair_me] = mix_send[c, pair_me]

    low_lanes = lax.broadcasted_iota(jnp.int32, (share_pad, LANES), 1) < rows
    for c in range(chunks):
        for copy in mix_copies[c]:
            copy.wait_recv()
        for pp in range(pair_n // 2):
            even = mix_held[c, 2 * pp].astype(jnp.float32)
            odd = mix_held[c, 2 * pp + 1].astype(jnp.float32)
            first = jnp.where(low_lanes, even, pltpu.roll(odd, rows, 1))
            second = jnp.where(low_lanes, pltpu.roll(even, rows, 1), odd)
            lhs_ref[2 * c, :, pp * LANES:(pp + 1) * LANES] = first.astype(jnp.bfloat16)
            lhs_ref[2 * c + 1, :, pp * LANES:(pp + 1) * LANES] = second.astype(jnp.bfloat16)

    for copy in place_copies + index_copies + sum(half_copies, []) + sum(mix_copies, []):
        copy.wait_send()


def product_kernel(share, lhs_ref, occ_rows_ref, vir_rows_ref, out_ref):
    step_i = pl.program_id(0)
    occ_total = occ_rows_ref.shape[1]
    items, share_pad, total_rows = lhs_ref.shape
    ones = lax.broadcasted_iota(jnp.int32, (occ_total, 2 * LANES), 0) == step_i
    chosen = jnp.where(ones, 1.0, 0.0).astype(jnp.bfloat16)
    occ_wide = jnp.dot(occ_rows_ref[...], chosen, preferred_element_type=jnp.float32).astype(jnp.bfloat16)
    lhs = lhs_ref[...].reshape(items * share_pad, total_rows)
    step = 2 * LANES
    for n in range(0, vir_rows_ref.shape[1], step):
        weights = occ_wide * vir_rows_ref[:, n:n + step]
        block = jnp.dot(lhs, weights, preferred_element_type=jnp.float32)
        for j in range(items):
            out_ref[j, :, n:n + step] = block[j * share_pad:j * share_pad + share]


def on_device(
    integrals, tile_pair, tile_lam, tile_count, mu_index, nu_index, occupied_coef, virtual_coef
):
    lam_n = lax.axis_size("lam")
    pair_n = lax.axis_size("pair")
    basis, occ_total = occupied_coef.shape
    vir_total = virtual_coef.shape[1]
    rows = mu_index.shape[0]
    slots, prows, blk = integrals.shape[1:4]
    bf16 = jnp.bfloat16
    both = LANES // rows
    occ_share = occ_total // lam_n
    chunks = occ_share // both
    share = vir_total // pair_n
    share_pad = round_up(share, ROW_TILE)
    duo = ROW_TILE // (both * prows)
    groups = slots // duo
    total_rows = rows * pair_n

    live = jnp.arange(slots, dtype=jnp.int32) < tile_count[0, 0]
    chosen = (tile_lam[0][:, None] == jnp.arange(basis // blk, dtype=jnp.int32)) & live[:, None]
    occ_tiles = jnp.einsum(
        "tl,lmj->tjm", chosen.astype(bf16), occupied_coef.reshape(basis // blk, blk, occ_total),
        preferred_element_type=jnp.float32,
    ).astype(bf16)
    factor = occ_tiles.reshape(groups, duo, lam_n * chunks, both, blk).transpose(0, 2, 3, 1, 4)
    same = (
        jnp.eye(duo, dtype=bool)[:, None, None, :, None] & jnp.eye(prows, dtype=bool)[None, None, :, None, :]
    )
    spread = jnp.where(
        same[None, None, :, :, :, :, :, None],
        factor[:, :, None, :, None, :, None, :],
        jnp.zeros((), bf16),
    ).reshape(groups, lam_n * chunks * ROW_TILE, duo * prows * blk)

    target = tile_pair[0][:, None] * prows + jnp.arange(prows, dtype=jnp.int32)
    hit = (target[:, None, :, None, None] == jnp.arange(rows, dtype=jnp.int32)) & jnp.eye(both, dtype=bool)[
        None, :, None, :, None
    ]
    place = hit.astype(bf16).reshape(slots * both * prows, LANES)
    index = jnp.broadcast_to(jnp.concatenate([mu_index, nu_index])[None, :], (8, 2 * rows))

    vmem = pl.BlockSpec(memory_space=pltpu.VMEM)
    hbm = pl.BlockSpec(memory_space=pl.ANY)
    dma = pltpu.SemaphoreType.DMA
    chunk_rows = slots * both * prows
    lhs, occ_rows, vir_rows = pl.pallas_call(
        functools.partial(exchange_kernel, lam_n, pair_n, chunks, share, share_pad, rows),
        out_shape=(
            jax.ShapeDtypeStruct((occ_share, share_pad, total_rows), bf16),
            jax.ShapeDtypeStruct((total_rows, occ_total), bf16),
            jax.ShapeDtypeStruct((total_rows, vir_total), bf16),
        ),
        in_specs=[hbm, vmem, vmem, vmem, vmem, hbm],
        out_specs=(vmem, vmem, vmem),
        scratch_shapes=[
            pltpu.VMEM((groups, duo * prows * blk, basis), bf16),
            pltpu.VMEM((basis, vir_total), bf16),
            pltpu.VMEM((lam_n, chunks, chunk_rows, basis), bf16),
            pltpu.VMEM((chunks, lam_n, chunk_rows, basis), bf16),
            pltpu.VMEM((lam_n, chunk_rows, LANES), bf16),
            pltpu.VMEM((pair_n, 8, LANES), jnp.int32),
            pltpu.VMEM((2, total_rows, basis), bf16),
            pltpu.VMEM((vir_total, LANES), jnp.float32),
            pltpu.VMEM((chunks, pair_n, share_pad, LANES), bf16),
            pltpu.VMEM((chunks, pair_n, share_pad, LANES), bf16),
            dma((groups,)),
            dma,
            dma((lam_n,)),
            dma((lam_n,)),
            dma((pair_n,)),
            dma((pair_n,)),
            dma((chunks, lam_n)),
            dma((chunks, lam_n)),
            dma((chunks, pair_n)),
            dma((chunks, pair_n)),
        ],
        compiler_params=pltpu.CompilerParams(
            collective_id=0, has_side_effects=True, vmem_limit_bytes=VMEM_BYTES
        ),
        name="exchange",
    )(integrals.reshape(slots * prows * blk, basis), spread, place, index, occupied_coef, virtual_coef)

    return pl.pallas_call(
        functools.partial(product_kernel, share),
        out_shape=jax.ShapeDtypeStruct((occ_share, share, occ_total * vir_total), jnp.float32),
        grid=(occ_total,),
        in_specs=[
            pl.BlockSpec((occ_share, share_pad, total_rows), lambda i: (0, 0, 0)),
            pl.BlockSpec((total_rows, occ_total), lambda i: (0, 0)),
            pl.BlockSpec((total_rows, vir_total), lambda i: (0, 0)),
        ],
        out_specs=pl.BlockSpec((occ_share, share, vir_total), lambda i: (0, 0, i)),
        compiler_params=pltpu.CompilerParams(vmem_limit_bytes=VMEM_BYTES),
        name="product",
    )(lhs, occ_rows, vir_rows)


def solution(mesh):
    placed = (
        P("pair", "lam", None, None, None),
        P("pair", "lam"),
        P("pair", "lam"),
        P("pair", "lam"),
        P("pair"),
        P("pair"),
        P(),
        P(),
    )
    return jax.shard_map(
        on_device, mesh=mesh, in_specs=placed, out_specs=P("lam", "pair", None), check_vma=False
    )
```

time: 354 us -> 67.5 us (0.19)
  blocking collectives: 173 us -> 0 us
  matrix products: 72.2 us -> 0.85 us
  local copies, waits for them, and re-layouts: 70.5 us -> 3.16 us
  Pallas kernels: 0 us -> 60.4 us
  loops' own time: 16.2 us -> 0 us
  other arithmetic: 17.5 us -> 1.8 us
  starting transfers between devices: 4.24 us -> 0 us
    psum x1 -> x0, blocking collectives: 158 us -> none  [on_device(): summed = lax.psum(partial_value, 'lam')]
    dot_general x9 -> x1, matrix products: 72.2 us -> 0.85 us  [on_device(): jnp.einsum('tl,lmj->tjm', chosen.astype(bf16), occupied_coef.reshape(basi...]
    pallas_call x0 -> x2, Pallas kernels: none -> 60.4 us  [the longest x1 35.3 us: on_device(): pl.pallas_call(functools.partial(exchange_kernel, lam_n, pair_n, chunks,...]
    convert_element_type x3 -> x1, local copies, waits for them, and re-layouts: 30.8 us -> 0.09 us  [on_device(): place = hit.astype(bf16).reshape(slots * both * prows, LANES)]
    convert_element_type x6 -> x1, other arithmetic: 17.4 us -> 0.1 us  [on_device(): place = hit.astype(bf16).reshape(slots * both * prows, LANES)]
    another operation x2 -> x0, loops' own time: 16.2 us -> none  [the longest x1 12.4 us: tile_pass(): return lax.fori_loop(0, live_total, add_tile, partial_value)]
    dynamic_slice x20 -> x0, local copies, waits for them, and re-layouts: 15.5 us -> none  [the longest x6 6.61 us: add_tile(): current = lax.dynamic_slice_in_dim(running, row_start, tile_rows, 1)]
    unnamed x1 -> x0, blocking collectives: 14.9 us -> none
  transfers between devices with their start and end apart: 1 -> 0, of which waited for: 0 -> 0; matrix products, arithmetic and copies ran while one was open for 1% -> 0% of each run, Pallas kernels for 0% -> 0%
where the time goes in v1:
time: 67.5 us; the launch traced here: 66.9 us
  Pallas kernels  60.4 us (89%)
  local copies, waits for them, and re-layouts  3.16 us (5%)
  other arithmetic  1.8 us (3%)
  matrix products  0.85 us (1%)
  between operations  0.73 us (1%)
    pallas_call x1, Pallas kernels, on_device(): pl.pallas_call(functools.partial(exchange_kernel, lam_n, pair_n, chunks,...  35.3 us
    pallas_call x1, Pallas kernels, on_device(): pl.pallas_call(functools.partial(product_kernel, share), out_shape=jax.Sh...  25 us

profile of v1, /device:TPU:0, one launch (start us, length us, event | category | flops | bytes accessed | tf_op | source)
XLA Modules:
  0.0 66.9 jit_solution(3014980422990260160)
XLA Ops:
  0.7 0.7 multiply_bitcast_fusion
  1.3 0.7 %pad_add_fusion = s32[128]{0:T(128)S(1)} fusion(s32[64]{0:T(128)} %param.13, s32[64]{0:T(128)} %param.12), kind=kLoop, calls=%fused_computation.13 | loop fusion | flops 128 | bytes 1024 | tf_op jit(solution)/shard_map/concatenate | solution.py:217
  2.1 0.1 broadcast_and_fusion
  2.2 0.1 iota_add_fusion
  2.2 0.1 iota_compare_fusion
  2.3 0.1 and_convert_fusion
  2.4 0.1 reshape.91.place_ref
  2.5 0.9 %reshape.89 = bf16[16,64,16]{1,0,2:T(8,128)(2,1)S(1)} reshape(bf16[1024,16]{0,1:T(8,128)(2,1)} %param.14) | data formatting | bytes 65536 | tf_op jit(solution)/shard_map/reshape | solution.py:199
  3.4 0.9 %convolution_convert_fusion = bf16[8,64,16]{1,0,2:T(8,128)(2,1)S(1)} fusion(bf16[16,64,16]{1,0,2:T(8,128)(2,1)S(1)} %reshape.89, s32[8]{0:T(128)} %bitcast.19, pred[8]{0:T(512)(128)(4,1)S(1)} %iota_compare_fusion.4), kind=kOutput, calls=%fused_computation | convolution fusion | flops 270592 | bytes 49192 | tf_op jit(solution)/shard_map/tl,lmj->tjm/dot_general | solution.py:198
  4.3 0.1 broadcast_in_dim.42
  4.4 0.2 broadcast_in_dim.43
  4.7 0.9 %copy.10.occ_ref = bf16[1024,16]{1,0:T(8,128)(2,1)S(1)} copy(bf16[1024,16]{0,1:T(8,128)(2,1)} %param.14) | data formatting | bytes 65536 | tf_op args[6]
  5.6 0.3 broadcast_in_dim.45
  5.9 0.6 broadcast_in_dim.46
  6.5 35.3 %exchange.1 = (bf16[4,160,512]{2,1,0:T(8,128)(2,1)S(1)}, bf16[512,16]{1,0:T(8,128)(2,1)S(1)}, bf16[512,1280]{1,0:T(8,128)(2,1)S(1)}) custom-call(bf16[2048,1024]{1,0:T(8,128)(2,1)} %bitcast.17, bf16[4,128,512]{2,1,0:T(8,128)(2,1)S(1)} %broadcast_select_fusion.spread_ref, bf16[64,128]{1,0:T(8,128)(2,1)S(1)} %reshape.91.place_ref, ...), custom_call_target="tpu_custom_call" | custom-call | tf_op jit(solution)/shard_map/exchange/pallas_call | solution.py:223
  41.9 25.0 %product.1 = f32[4,160,20480]{2,1,0:T(8,128)} custom-call(bf16[4,160,512]{2,1,0:T(8,128)(2,1)S(1)} %get-tuple-element.8.lhs_ref, bf16[512,16]{1,0:T(8,128)(2,1)S(1)} %get-tuple-element.9.occ_rows_ref, bf16[512,1280]{1,0:T(8,128)(2,1)S(1)} %get-tuple-element.10.vir_rows_ref), custom_call_target="tpu_custom_call" | custom-call | tf_op jit(solution)/shard_map/product/pallas_call | solution.py:260
  (6 shorter events, 0.1 us)

commit v2 on v1

--- a/solution.py
+++ b/solution.py
@@ -17,11 +17,29 @@
     return (value + step - 1) // step * step
 
 
+def bits_of(size):
+    return size.bit_length() - 1
+
+
+def split_iota(shape, dim, *sizes):
+    left = lax.broadcasted_iota(jnp.int32, shape, dim)
+    parts = []
+    for size in reversed(sizes):
+        parts.append(left & (size - 1))
+        left = left >> bits_of(size)
+    return [left] + parts[::-1]
+
+
+def one_hot(hit):
+    return jnp.where(hit, 1.0, 0.0).astype(jnp.bfloat16)
+
+
 def exchange_kernel(
-    lam_n, pair_n, chunks, share, share_pad, rows,
-    tiles_ref, spread_ref, place_ref, index_ref, occ_ref, vir_ref,
-    lhs_ref, occ_rows_ref, vir_rows_ref,
-    tile_buf, vir_buf, half_send, half_held, place_held, index_held, pick, mixed_t, mix_send, mix_held,
+    lam_n, pair_n, chunks, share, share_pad, rows, prows, blk,
+    tiles_ref, pair_ref, lam_ref, count_ref, mu_ref, nu_ref, occ_ref, vir_ref,
+    lhs_ref, occ_wide_ref, vir_rows_ref,
+    tile_buf, vir_buf, place_ref, index_ref, half_send, half_held, place_held, index_held, pick, mixed_t,
+    mix_send, mix_held,
     tile_sem, vir_sem, place_ssem, place_rsem, index_ssem, index_rsem,
     half_ssem, half_rsem, mix_ssem, mix_rsem,
 ):
@@ -30,6 +48,10 @@
     groups = tile_buf.shape[0]
     depth = tile_buf.shape[1]
     basis = vir_buf.shape[0]
+    occ_total = occ_ref.shape[0]
+    both = LANES // rows
+    slots = pair_ref.shape[1]
+    duo = slots // groups
 
     barrier = pltpu.get_barrier_semaphore()
     for d in range(1, lam_n):
@@ -46,9 +68,40 @@
         copy.start()
     vir_copy.start()
 
+    slot, row_j, row_k = split_iota((slots * both * prows, LANES), 0, both, prows)
+    lane_j, lane_r = split_iota((slots * both * prows, LANES), 1, rows)
+    goal = jnp.zeros_like(slot)
+    for t in range(slots):
+        goal = jnp.where(slot == t, pair_ref[0, t], goal)
+    place_ref[...] = one_hot((row_j == lane_j) & (lane_r == goal * prows + row_k))
+    index_ref[...] = jnp.zeros_like(index_ref)
+    index_ref[0:1, 0:rows] = mu_ref[...]
+    index_ref[1:2, 0:rows] = nu_ref[...]
+
+    lam_rows = basis // lam_n
+    width = slots * prows * blk
+    lane_t, _, lane_m = split_iota((1, width), 1, prows, blk)
+    source = jnp.zeros_like(lane_t)
+    for t in range(slots):
+        first = jnp.where(count_ref[0, 0] > t, lam_ref[0, t] * blk - lam_me * lam_rows, -2 * basis)
+        source = jnp.where(lane_t == t, first, source)
+    source = source + lane_m
+    chosen = one_hot(lax.broadcasted_iota(jnp.int32, (lam_rows, width), 0) == source)
+    occ_own = occ_ref[:, pl.ds(pl.multiple_of(lam_me * lam_rows, lam_rows), lam_rows)]
+    occ_tiles = jnp.dot(occ_own, chosen, preferred_element_type=jnp.float32).astype(jnp.bfloat16)
+    height = lam_n * chunks * ROW_TILE
+    group, _, repeat_j, _ = split_iota((height, occ_total), 0, duo, both, prows)
+    repeat = one_hot(lax.broadcasted_iota(jnp.int32, (height, occ_total), 1) == group * both + repeat_j)
+    factor = jnp.dot(repeat, occ_tiles, preferred_element_type=jnp.float32)
+    _, row_t, _, row_k = split_iota((height, width), 0, duo, both, prows)
+    lane_t, lane_k, _ = split_iota((height, width), 1, prows, blk)
+    spread = jnp.where((row_t == (lane_t & (duo - 1))) & (row_k == lane_k), factor, 0.0).astype(jnp.bfloat16)
+
     for q in range(groups):
         tile_copies[q].wait()
-        part = jnp.dot(spread_ref[q], tile_buf[q], preferred_element_type=jnp.float32).astype(jnp.bfloat16)
+        part = jnp.dot(
+            spread[:, q * depth:(q + 1) * depth], tile_buf[q], preferred_element_type=jnp.float32
+        ).astype(jnp.bfloat16)
         for g in range(lam_n * chunks):
             half_send[g // chunks, g % chunks, q * ROW_TILE:(q + 1) * ROW_TILE, :] = part[
                 g * ROW_TILE:(g + 1) * ROW_TILE
@@ -97,14 +150,21 @@
     for copy in index_copies:
         copy.wait_recv()
     for p in range(pair_n):
-        line = index_held[p, 0:1, :].astype(jnp.float32)
+        named = index_held[p].astype(jnp.float32)
+        low = lax.broadcasted_iota(jnp.int32, (1, LANES), 1) < rows
+        line = jnp.where(low, named[0:1], pltpu.roll(named, rows, 1)[1:2])
         column = jnp.transpose(jnp.broadcast_to(line, (LANES, LANES)))
         for b in range(basis // LANES):
             name = (lax.broadcasted_iota(jnp.int32, (LANES, LANES), 1) + b * LANES).astype(jnp.float32)
-            hit = jnp.where(column == name, 1.0, 0.0).astype(jnp.bfloat16)
+            hit = one_hot(column == name)
             pick[0, p * rows:(p + 1) * rows, b * LANES:(b + 1) * LANES] = hit[:rows]
             pick[1, p * rows:(p + 1) * rows, b * LANES:(b + 1) * LANES] = hit[rows:]
-    occ_rows_ref[...] = jnp.dot(pick[0], occ_ref[...], preferred_element_type=jnp.float32).astype(jnp.bfloat16)
+    occ_rows = lax.dot_general(
+        pick[0], occ_ref[...], (((1,), (1,)), ((), ())), preferred_element_type=jnp.float32
+    ).astype(jnp.bfloat16)
+    lane_i, _ = split_iota((occ_total, occ_total * LANES), 1, LANES)
+    widen = one_hot(lax.broadcasted_iota(jnp.int32, lane_i.shape, 0) == lane_i)
+    occ_wide_ref[...] = jnp.dot(occ_rows, widen, preferred_element_type=jnp.float32).astype(jnp.bfloat16)
     vir_copy.wait()
     step = 2 * LANES
     for n in range(0, vir_buf.shape[1], step):
@@ -158,13 +218,9 @@
         copy.wait_send()
 
 
-def product_kernel(share, lhs_ref, occ_rows_ref, vir_rows_ref, out_ref):
-    step_i = pl.program_id(0)
-    occ_total = occ_rows_ref.shape[1]
+def product_kernel(share, lhs_ref, occ_wide_ref, vir_rows_ref, out_ref):
     items, share_pad, total_rows = lhs_ref.shape
-    ones = lax.broadcasted_iota(jnp.int32, (occ_total, 2 * LANES), 0) == step_i
-    chosen = jnp.where(ones, 1.0, 0.0).astype(jnp.bfloat16)
-    occ_wide = jnp.dot(occ_rows_ref[...], chosen, preferred_element_type=jnp.float32).astype(jnp.bfloat16)
+    occ_wide = jnp.concatenate([occ_wide_ref[...]] * 2, axis=1)
     lhs = lhs_ref[...].reshape(items * share_pad, total_rows)
     step = 2 * LANES
     for n in range(0, vir_rows_ref.shape[1], step):
@@ -193,45 +249,25 @@
     groups = slots // duo
     total_rows = rows * pair_n
 
-    live = jnp.arange(slots, dtype=jnp.int32) < tile_count[0, 0]
-    chosen = (tile_lam[0][:, None] == jnp.arange(basis // blk, dtype=jnp.int32)) & live[:, None]
-    occ_tiles = jnp.einsum(
-        "tl,lmj->tjm", chosen.astype(bf16), occupied_coef.reshape(basis // blk, blk, occ_total),
-        preferred_element_type=jnp.float32,
-    ).astype(bf16)
-    factor = occ_tiles.reshape(groups, duo, lam_n * chunks, both, blk).transpose(0, 2, 3, 1, 4)
-    same = (
-        jnp.eye(duo, dtype=bool)[:, None, None, :, None] & jnp.eye(prows, dtype=bool)[None, None, :, None, :]
-    )
-    spread = jnp.where(
-        same[None, None, :, :, :, :, :, None],
-        factor[:, :, None, :, None, :, None, :],
-        jnp.zeros((), bf16),
-    ).reshape(groups, lam_n * chunks * ROW_TILE, duo * prows * blk)
-
-    target = tile_pair[0][:, None] * prows + jnp.arange(prows, dtype=jnp.int32)
-    hit = (target[:, None, :, None, None] == jnp.arange(rows, dtype=jnp.int32)) & jnp.eye(both, dtype=bool)[
-        None, :, None, :, None
-    ]
-    place = hit.astype(bf16).reshape(slots * both * prows, LANES)
-    index = jnp.broadcast_to(jnp.concatenate([mu_index, nu_index])[None, :], (8, 2 * rows))
-
     vmem = pl.BlockSpec(memory_space=pltpu.VMEM)
+    smem = pl.BlockSpec(memory_space=pltpu.SMEM)
     hbm = pl.BlockSpec(memory_space=pl.ANY)
     dma = pltpu.SemaphoreType.DMA
     chunk_rows = slots * both * prows
-    lhs, occ_rows, vir_rows = pl.pallas_call(
-        functools.partial(exchange_kernel, lam_n, pair_n, chunks, share, share_pad, rows),
+    lhs, occ_wide, vir_rows = pl.pallas_call(
+        functools.partial(exchange_kernel, lam_n, pair_n, chunks, share, share_pad, rows, prows, blk),
         out_shape=(
             jax.ShapeDtypeStruct((occ_share, share_pad, total_rows), bf16),
-            jax.ShapeDtypeStruct((total_rows, occ_total), bf16),
+            jax.ShapeDtypeStruct((total_rows, occ_total * LANES), bf16),
             jax.ShapeDtypeStruct((total_rows, vir_total), bf16),
         ),
-        in_specs=[hbm, vmem, vmem, vmem, vmem, hbm],
+        in_specs=[hbm, smem, smem, smem, vmem, vmem, vmem, hbm],
         out_specs=(vmem, vmem, vmem),
         scratch_shapes=[
             pltpu.VMEM((groups, duo * prows * blk, basis), bf16),
             pltpu.VMEM((basis, vir_total), bf16),
+            pltpu.VMEM((chunk_rows, LANES), bf16),
+            pltpu.VMEM((8, LANES), jnp.int32),
             pltpu.VMEM((lam_n, chunks, chunk_rows, basis), bf16),
             pltpu.VMEM((chunks, lam_n, chunk_rows, basis), bf16),
             pltpu.VMEM((lam_n, chunk_rows, LANES), bf16),
@@ -255,7 +291,10 @@
             collective_id=0, has_side_effects=True, vmem_limit_bytes=VMEM_BYTES
         ),
         name="exchange",
-    )(integrals.reshape(slots * prows * blk, basis), spread, place, index, occupied_coef, virtual_coef)
+    )(
+        integrals.reshape(slots * prows * blk, basis), tile_pair, tile_lam, tile_count,
+        mu_index[None, :], nu_index[None, :], occupied_coef.T, virtual_coef,
+    )
 
     return pl.pallas_call(
         functools.partial(product_kernel, share),
@@ -263,13 +302,13 @@
         grid=(occ_total,),
         in_specs=[
             pl.BlockSpec((occ_share, share_pad, total_rows), lambda i: (0, 0, 0)),
-            pl.BlockSpec((total_rows, occ_total), lambda i: (0, 0)),
+            pl.BlockSpec((total_rows, LANES), lambda i: (0, i)),
             pl.BlockSpec((total_rows, vir_total), lambda i: (0, 0)),
         ],
         out_specs=pl.BlockSpec((occ_share, share, vir_total), lambda i: (0, 0, i)),
         compiler_params=pltpu.CompilerParams(vmem_limit_bytes=VMEM_BYTES),
         name="product",
-    )(lhs, occ_rows, vir_rows)
+    )(lhs, occ_wide, vir_rows)
 
 
 def solution(mesh):

time: 67.5 us -> 64.5 us (0.956)
  other arithmetic: 1.8 us -> 0 us
  matrix products: 0.85 us -> 0 us
    unnamed x1 -> x10, local copies, waits for them, and re-layouts: 0.93 us -> 3.37 us
    pallas_call x1, Pallas kernels: 25 us -> 23.2 us  [on_device(): pl.pallas_call(functools.partial(product_kernel, share), out_shape=jax.Sh...]
    pallas_call x1, Pallas kernels: 35.3 us -> 36.7 us  [on_device(): pl.pallas_call(functools.partial(exchange_kernel, lam_n, pair_n, chunks,...]
    broadcast_in_dim x5 -> x0, local copies, waits for them, and re-layouts: 1.24 us -> none  [the longest x4 1.24 us: on_device(): jnp.where(same[None, None, :, :, :, :, :, None], factor[:, :, None, :, No...]
    reshape x1 -> x0, local copies, waits for them, and re-layouts: 0.88 us -> none  [on_device(): occupied_coef.reshape(basis // blk, blk, occ_total)]
    dot_general x1 -> x0, matrix products: 0.85 us -> none  [on_device(): jnp.einsum('tl,lmj->tjm', chosen.astype(bf16), occupied_coef.reshape(basi...]
    concatenate x1 -> x0, other arithmetic: 0.75 us -> none  [on_device(): jnp.concatenate([mu_index, nu_index])[None, :]]
where the time goes in v2:
time: 64.5 us; the launch traced here: 64 us
  Pallas kernels  59.9 us (93%)
  local copies, waits for them, and re-layouts  3.37 us (5%)
  between operations  0.67 us (1%)
    pallas_call x1, Pallas kernels, on_device(): pl.pallas_call(functools.partial(exchange_kernel, lam_n, pair_n, chunks,...  36.7 us
    pallas_call x1, Pallas kernels, on_device(): pl.pallas_call(functools.partial(product_kernel, share), out_shape=jax.Sh...  23.2 us
    unnamed x10, local copies, waits for them, and re-layouts  3.37 us

profile of v2, /device:TPU:0, one launch (start us, length us, event | category | flops | bytes accessed | tf_op | source)
XLA Modules:
  0.0 64.0 jit_solution(7322518594033952071)
XLA Ops:
  0.7 0.0 copy-start
  0.7 0.7 %copy-done = bf16[1024,16]{0,1:T(8,128)(2,1)S(1)} copy-done((bf16[1024,16]{0,1:T(8,128)(2,1)S(1)}, bf16[1024,16]{0,1:T(8,128)(2,1)}, u32[]{:S(2)}) %copy-start) | copy-done | bytes 32792
  1.4 0.0 copy-start.1
  1.4 0.7 %copy-done.1 = s32[1,8]{1,0:T(1,128)S(1)} copy-done((s32[1,8]{1,0:T(1,128)S(1)}, s32[1,8]{1,0:T(1,128)}, u32[]{:S(2)}) %copy-start.1) | copy-done | bytes 56
  2.1 0.0 copy-start.2
  2.1 0.7 %copy-done.2 = s32[1,8]{1,0:T(1,128)S(1)} copy-done((s32[1,8]{1,0:T(1,128)S(1)}, s32[1,8]{1,0:T(1,128)}, u32[]{:S(2)}) %copy-start.2) | copy-done | bytes 56
  2.7 0.0 copy-start.3
  2.7 0.7 %copy-done.3 = s32[64]{0:T(128)S(1)} copy-done((s32[64]{0:T(128)S(1)}, s32[64]{0:T(128)}, u32[]{:S(2)}) %copy-start.3) | copy-done | bytes 280
  3.4 0.0 copy-start.4
  3.4 0.7 %copy-done.4 = s32[64]{0:T(128)S(1)} copy-done((s32[64]{0:T(128)S(1)}, s32[64]{0:T(128)}, u32[]{:S(2)}) %copy-start.4) | copy-done | bytes 280
  4.0 36.7 %exchange.1 = (bf16[4,160,512]{2,1,0:T(8,128)(2,1)S(1)}, bf16[512,2048]{1,0:T(8,128)(2,1)S(1)}, bf16[512,1280]{1,0:T(8,128)(2,1)S(1)}) custom-call(bf16[2048,1024]{1,0:T(8,128)(2,1)} %bitcast.7, s32[1,8]{1,0:T(1,128)S(1)} %copy-done.1, s32[1,8]{1,0:T(1,128)S(1)} %copy-done.2, s32[1,1]{1,0:T(1,128)S(6)} %copy.9.count_ref, s32[1,64]{1,0:T(1,128)S(1)} %bitcast.5, ...), custom_call_target="tpu_custom_call" | custom-call | tf_op jit(solution)/shard_map/exchange/pallas_call | solution.py:257
  40.8 23.2 %product.1 = f32[4,160,20480]{2,1,0:T(8,128)} custom-call(bf16[4,160,512]{2,1,0:T(8,128)(2,1)S(1)} %get-tuple-element.8.lhs_ref, bf16[512,2048]{1,0:T(8,128)(2,1)S(1)} %get-tuple-element.9.occ_wide_ref, bf16[512,1280]{1,0:T(8,128)(2,1)S(1)} %get-tuple-element.10.vir_rows_ref), custom_call_target="tpu_custom_call" | custom-call | tf_op jit(solution)/shard_map/product/pallas_call | solution.py:299
Async XLA Ops:
  0.7 0.8 %copy-start = (bf16[1024,16]{0,1:T(8,128)(2,1)S(1)}, bf16[1024,16]{0,1:T(8,128)(2,1)}, u32[]{:S(2)}) copy-start(bf16[1024,16]{0,1:T(8,128)(2,1)} %param.14) | copy-start | bytes 98308
  1.4 0.7 %copy-start.1 = (s32[1,8]{1,0:T(1,128)S(1)}, s32[1,8]{1,0:T(1,128)}, u32[]{:S(2)}) copy-start(s32[1,8]{1,0:T(1,128)} %pair_ref.1) | copy-start | bytes 100
  2.1 0.7 %copy-start.2 = (s32[1,8]{1,0:T(1,128)S(1)}, s32[1,8]{1,0:T(1,128)}, u32[]{:S(2)}) copy-start(s32[1,8]{1,0:T(1,128)} %lam_ref.1) | copy-start | bytes 100
  2.7 0.7 %copy-start.3 = (s32[64]{0:T(128)S(1)}, s32[64]{0:T(128)}, u32[]{:S(2)}) copy-start(s32[64]{0:T(128)} %param.12) | copy-start | bytes 772
  3.4 0.7 %copy-start.4 = (s32[64]{0:T(128)S(1)}, s32[64]{0:T(128)}, u32[]{:S(2)}) copy-start(s32[64]{0:T(128)} %param.13) | copy-start | bytes 772

commit v3 on v2

--- a/solution.py
+++ b/solution.py
@@ -9,7 +9,7 @@
 
 LANES = 128
 ROW_TILE = 16
-VMEM_BYTES = 50 * 1024 * 1024
+VMEM_BYTES = 64 * 1024 * 1024
 MESH = pl.DeviceIdType.MESH
 
 
@@ -36,8 +36,10 @@
 
 def exchange_kernel(
     lam_n, pair_n, chunks, share, share_pad, rows, prows, blk,
-    tiles_ref, pair_ref, lam_ref, count_ref, mu_ref, nu_ref, occ_ref, vir_ref,
-    lhs_ref, occ_wide_ref, vir_rows_ref,
+    tiles_ref, pair_hbm, lam_hbm, count_hbm, mu_hbm, nu_hbm, occ_hbm, vir_ref,
+    lhs_out, occ_wide_out, vir_rows_out,
+    lhs_ref, occ_wide_ref, vir_rows_ref, out_sem,
+    pair_ref, lam_ref, count_ref, mu_ref, nu_ref, occ_ref, small_sem,
     tile_buf, vir_buf, place_ref, index_ref, half_send, half_held, place_held, index_held, pick, mixed_t,
     mix_send, mix_held,
     tile_sem, vir_sem, place_ssem, place_rsem, index_ssem, index_rsem,
@@ -59,6 +61,15 @@
     for d in range(1, pair_n):
         pl.semaphore_signal(barrier, inc=1, device_id={"pair": lax.rem(pair_me + d, pair_n)}, device_id_type=MESH)
 
+    small_copies = [
+        pltpu.make_async_copy(source, target, small_sem.at[n])
+        for n, (source, target) in enumerate([
+            (pair_hbm, pair_ref), (lam_hbm, lam_ref), (count_hbm, count_ref),
+            (mu_hbm, mu_ref), (nu_hbm, nu_ref), (occ_hbm, occ_ref),
+        ])
+    ]
+    for copy in small_copies:
+        copy.start()
     tile_copies = [
         pltpu.make_async_copy(tiles_ref.at[pl.ds(q * depth, depth)], tile_buf.at[q], tile_sem.at[q])
         for q in range(groups)
@@ -67,6 +78,9 @@
     for copy in tile_copies:
         copy.start()
     vir_copy.start()
+
+    for copy in small_copies:
+        copy.wait()
 
     slot, row_j, row_k = split_iota((slots * both * prows, LANES), 0, both, prows)
     lane_j, lane_r = split_iota((slots * both * prows, LANES), 1, rows)
@@ -171,6 +185,13 @@
         vir_rows_ref[:, n:n + step] = jnp.dot(
             pick[1], vir_buf[:, n:n + step], preferred_element_type=jnp.float32
         ).astype(jnp.bfloat16)
+
+    out_copies = [
+        pltpu.make_async_copy(occ_wide_ref, occ_wide_out, out_sem.at[0]),
+        pltpu.make_async_copy(vir_rows_ref, vir_rows_out, out_sem.at[1]),
+    ]
+    for copy in out_copies:
+        copy.start()
 
     for copy in place_copies:
         copy.wait_recv()
@@ -213,21 +234,61 @@
             second = jnp.where(low_lanes, pltpu.roll(even, rows, 1), odd)
             lhs_ref[2 * c, :, pp * LANES:(pp + 1) * LANES] = first.astype(jnp.bfloat16)
             lhs_ref[2 * c + 1, :, pp * LANES:(pp + 1) * LANES] = second.astype(jnp.bfloat16)
+        copy = pltpu.make_async_copy(
+            lhs_ref.at[pl.ds(2 * c, 2)], lhs_out.at[pl.ds(2 * c, 2)], out_sem.at[2 + c]
+        )
+        copy.start()
+        out_copies.append(copy)
 
     for copy in place_copies + index_copies + sum(half_copies, []) + sum(mix_copies, []):
         copy.wait_send()
-
-
-def product_kernel(share, lhs_ref, occ_wide_ref, vir_rows_ref, out_ref):
+    for copy in out_copies:
+        copy.wait()
+
+
+def product_kernel(share, lhs_ref, occ_wide_ref, vir_rows_ref, out_ref, held, sems):
     items, share_pad, total_rows = lhs_ref.shape
+    vir_total = vir_rows_ref.shape[1]
+    step_i = pl.program_id(0)
+    last = pl.num_programs(0) - 1
+    step = 2 * LANES
+    middle = round_up(vir_total // 2, step)
+    parts = ((0, middle), (middle, vir_total))
+
+    def copies(at, part):
+        begin, end = parts[part]
+        slot = lax.rem(at, 2)
+        columns = pl.ds(pl.multiple_of(at * vir_total + begin, LANES), end - begin)
+        return [
+            pltpu.make_async_copy(
+                held.at[slot, j, :, pl.ds(begin, end - begin)], out_ref.at[j, :, columns], sems.at[slot, part, j]
+            )
+            for j in range(items)
+        ]
+
+    @pl.when(step_i >= 2)
+    def _():
+        for part in range(2):
+            for copy in copies(step_i - 2, part):
+                copy.wait()
+
+    slot_now = lax.rem(step_i, 2)
     occ_wide = jnp.concatenate([occ_wide_ref[...]] * 2, axis=1)
     lhs = lhs_ref[...].reshape(items * share_pad, total_rows)
-    step = 2 * LANES
-    for n in range(0, vir_rows_ref.shape[1], step):
-        weights = occ_wide * vir_rows_ref[:, n:n + step]
-        block = jnp.dot(lhs, weights, preferred_element_type=jnp.float32)
-        for j in range(items):
-            out_ref[j, :, n:n + step] = block[j * share_pad:j * share_pad + share]
+    for part in range(2):
+        for n in range(*parts[part], step):
+            weights = occ_wide * vir_rows_ref[:, n:n + step]
+            block = jnp.dot(lhs, weights, preferred_element_type=jnp.float32)
+            held[slot_now, :, :, n:n + step] = block.reshape(items, share_pad, step)[:, :share]
+        for copy in copies(step_i, part):
+            copy.start()
+
+    @pl.when(step_i == last)
+    def _():
+        for at in (last - 1, last):
+            for part in range(2):
+                for copy in copies(at, part):
+                    copy.wait()
 
 
 def on_device(
@@ -249,9 +310,7 @@
     groups = slots // duo
     total_rows = rows * pair_n
 
-    vmem = pl.BlockSpec(memory_space=pltpu.VMEM)
-    smem = pl.BlockSpec(memory_space=pltpu.SMEM)
-    hbm = pl.BlockSpec(memory_space=pl.ANY)
+    pinned = pl.BlockSpec(memory_space=pltpu.HBM)
     dma = pltpu.SemaphoreType.DMA
     chunk_rows = slots * both * prows
     lhs, occ_wide, vir_rows = pl.pallas_call(
@@ -261,9 +320,20 @@
             jax.ShapeDtypeStruct((total_rows, occ_total * LANES), bf16),
             jax.ShapeDtypeStruct((total_rows, vir_total), bf16),
         ),
-        in_specs=[hbm, smem, smem, smem, vmem, vmem, vmem, hbm],
-        out_specs=(vmem, vmem, vmem),
+        in_specs=[pinned] * 8,
+        out_specs=(pinned, pinned, pinned),
         scratch_shapes=[
+            pltpu.VMEM((occ_share, share_pad, total_rows), bf16),
+            pltpu.VMEM((total_rows, occ_total * LANES), bf16),
+            pltpu.VMEM((total_rows, vir_total), bf16),
+            dma((2 + chunks,)),
+            pltpu.SMEM((1, slots), jnp.int32),
+            pltpu.SMEM((1, slots), jnp.int32),
+            pltpu.SMEM((1, 1), jnp.int32),
+            pltpu.VMEM((1, rows), jnp.int32),
+            pltpu.VMEM((1, rows), jnp.int32),
+            pltpu.VMEM((occ_total, basis), bf16),
+            dma((6,)),
             pltpu.VMEM((groups, duo * prows * blk, basis), bf16),
             pltpu.VMEM((basis, vir_total), bf16),
             pltpu.VMEM((chunk_rows, LANES), bf16),
@@ -305,7 +375,11 @@
             pl.BlockSpec((total_rows, LANES), lambda i: (0, i)),
             pl.BlockSpec((total_rows, vir_total), lambda i: (0, 0)),
         ],
-        out_specs=pl.BlockSpec((occ_share, share, vir_total), lambda i: (0, 0, i)),
+        out_specs=pl.BlockSpec(memory_space=pl.ANY),
+        scratch_shapes=[
+            pltpu.VMEM((2, occ_share, share, vir_total), jnp.float32),
+            dma((2, 2, occ_share)),
+        ],
         compiler_params=pltpu.CompilerParams(vmem_limit_bytes=VMEM_BYTES),
         name="product",
     )(lhs, occ_wide, vir_rows)

time: 64.5 us -> 59.6 us (0.924)
  local copies, waits for them, and re-layouts: 3.37 us -> 0 us
  Pallas kernels: 59.9 us -> 58.4 us
    unnamed x10 -> x0, local copies, waits for them, and re-layouts: 3.37 us -> none
    pallas_call x1, Pallas kernels: 23.2 us -> 21.2 us  [on_device(): pl.pallas_call(functools.partial(product_kernel, share), out_shape=jax.Sh...]
where the time goes in v3:
time: 59.6 us; the launch traced here: 59 us
  Pallas kernels  58.4 us (98%)
  between operations  0.66 us (1%)
    pallas_call x1, Pallas kernels, on_device(): pl.pallas_call(functools.partial(exchange_kernel, lam_n, pair_n, chunks,...  37.2 us
    pallas_call x1, Pallas kernels, on_device(): pl.pallas_call(functools.partial(product_kernel, share), out_shape=jax.Sh...  21.2 us

profile of v3, /device:TPU:0, one launch (start us, length us, event | category | flops | bytes accessed | tf_op | source)
XLA Modules:
  0.0 59.0 jit_solution(12444843749928410997)
XLA Ops:
  0.7 37.2 %exchange.1 = (bf16[4,160,512]{2,1,0:T(8,128)(2,1)}, bf16[512,2048]{1,0:T(8,128)(2,1)}, bf16[512,1280]{1,0:T(8,128)(2,1)}) custom-call(bf16[2048,1024]{1,0:T(8,128)(2,1)} %bitcast.4, s32[1,8]{1,0:T(1,128)} %pair_hbm.1, s32[1,8]{1,0:T(1,128)} %lam_hbm.1, s32[1,1]{1,0:T(1,128)S(6)} %copy.9.count_hbm, s32[1,64]{1,0:T(1,128)} %bitcast.6, s32[1,64]{1,0:T(1,128)} %bitcast.7, ...), custom_call_target="tpu_custom_call" | custom-call | tf_op jit(solution)/shard_map/exchange/pallas_call | solution.py:316
  37.8 21.2 %product.1 = f32[4,160,20480]{2,1,0:T(8,128)} custom-call(bf16[4,160,512]{2,1,0:T(8,128)(2,1)} %get-tuple-element.8.lhs_ref, bf16[512,2048]{1,0:T(8,128)(2,1)} %get-tuple-element.9.occ_wide_ref, bf16[512,1280]{1,0:T(8,128)(2,1)} %get-tuple-element.10.vir_rows_ref), custom_call_target="tpu_custom_call" | custom-call | tf_op jit(solution)/shard_map/product/pallas_call | solution.py:369

commit v4 on v3

--- a/solution.py
+++ b/solution.py
@@ -123,7 +123,6 @@
 
     pl.semaphore_wait(barrier, lam_n + pair_n - 2)
 
-    sends = []
     place_copies, index_copies, half_copies, mix_copies = [], [], [], []
     for d in range(1, lam_n):
         peer = lax.rem(lam_me + d, lam_n)
@@ -143,9 +142,9 @@
         )
         copy.start()
         index_copies.append(copy)
-    for c in range(chunks):
+    def send_half(c):
         row_copies = []
-        for d in range(1, lam_n):
+        for d in range(lam_n - 1, 0, -1):
             peer = lax.rem(lam_me + d, lam_n)
             copy = pltpu.make_async_remote_copy(
                 src_ref=half_send.at[peer, c], dst_ref=half_held.at[c, lam_me],
@@ -156,6 +155,7 @@
             row_copies.append(copy)
         half_copies.append(row_copies)
 
+    send_half(0)
     place_held[lam_me] = place_ref[...]
     index_held[pair_me] = index_ref[...]
     for c in range(chunks):
@@ -192,6 +192,11 @@
     ]
     for copy in out_copies:
         copy.start()
+
+    for c in range(1, chunks):
+        for copy in half_copies[c - 1]:
+            copy.wait_send()
+        send_half(c)
 
     for copy in place_copies:
         copy.wait_recv()
@@ -240,7 +245,7 @@
         copy.start()
         out_copies.append(copy)
 
-    for copy in place_copies + index_copies + sum(half_copies, []) + sum(mix_copies, []):
+    for copy in place_copies + index_copies + half_copies[-1] + sum(mix_copies, []):
         copy.wait_send()
     for copy in out_copies:
         copy.wait()
@@ -273,13 +278,13 @@
                 copy.wait()
 
     slot_now = lax.rem(step_i, 2)
-    occ_wide = jnp.concatenate([occ_wide_ref[...]] * 2, axis=1)
     lhs = lhs_ref[...].reshape(items * share_pad, total_rows)
     for part in range(2):
-        for n in range(*parts[part], step):
-            weights = occ_wide * vir_rows_ref[:, n:n + step]
-            block = jnp.dot(lhs, weights, preferred_element_type=jnp.float32)
-            held[slot_now, :, :, n:n + step] = block.reshape(items, share_pad, step)[:, :share]
+        begin, end = parts[part]
+        occ_wide = jnp.concatenate([occ_wide_ref[...]] * ((end - begin) // LANES), axis=1)
+        weights = occ_wide * vir_rows_ref[:, begin:end]
+        block = jnp.dot(lhs, weights, preferred_element_type=jnp.float32)
+        held[slot_now, :, :, begin:end] = block.reshape(items, share_pad, end - begin)[:, :share]
         for copy in copies(step_i, part):
             copy.start()
 

time: 59.6 us -> 63.1 us (1.059)
  Pallas kernels: 58.4 us -> 62.1 us
    pallas_call x1, Pallas kernels: 37.2 us -> 40.9 us  [on_device(): pl.pallas_call(functools.partial(exchange_kernel, lam_n, pair_n, chunks,...]
where the time goes in v4:
time: 63.1 us; the launch traced here: 62.8 us
  Pallas kernels  62.1 us (98%)
  between operations  0.66 us (1%)
    pallas_call x1, Pallas kernels, on_device(): pl.pallas_call(functools.partial(exchange_kernel, lam_n, pair_n, chunks,...  40.9 us
    pallas_call x1, Pallas kernels, on_device(): pl.pallas_call(functools.partial(product_kernel, share), out_shape=jax.Sh...  21.2 us

profile of v4, /device:TPU:0, one launch (start us, length us, event | category | flops | bytes accessed | tf_op | source)
XLA Modules:
  0.0 62.8 jit_solution(17825183110970699358)
XLA Ops:
  0.7 40.9 %exchange.1 = (bf16[4,160,512]{2,1,0:T(8,128)(2,1)}, bf16[512,2048]{1,0:T(8,128)(2,1)}, bf16[512,1280]{1,0:T(8,128)(2,1)}) custom-call(bf16[2048,1024]{1,0:T(8,128)(2,1)} %bitcast.4, s32[1,8]{1,0:T(1,128)} %pair_hbm.1, s32[1,8]{1,0:T(1,128)} %lam_hbm.1, s32[1,1]{1,0:T(1,128)S(6)} %copy.9.count_hbm, s32[1,64]{1,0:T(1,128)} %bitcast.6, s32[1,64]{1,0:T(1,128)} %bitcast.7, ...), custom_call_target="tpu_custom_call" | custom-call | tf_op jit(solution)/shard_map/exchange/pallas_call | solution.py:321
  41.6 21.2 %product.1 = f32[4,160,20480]{2,1,0:T(8,128)} custom-call(bf16[4,160,512]{2,1,0:T(8,128)(2,1)} %get-tuple-element.8.lhs_ref, bf16[512,2048]{1,0:T(8,128)(2,1)} %get-tuple-element.9.occ_wide_ref, bf16[512,1280]{1,0:T(8,128)(2,1)} %get-tuple-element.10.vir_rows_ref), custom_call_target="tpu_custom_call" | custom-call | tf_op jit(solution)/shard_map/product/pallas_call | solution.py:374

commit v5 on v3

--- a/solution.py
+++ b/solution.py
@@ -111,6 +111,22 @@
     lane_t, lane_k, _ = split_iota((height, width), 1, prows, blk)
     spread = jnp.where((row_t == (lane_t & (duo - 1))) & (row_k == lane_k), factor, 0.0).astype(jnp.bfloat16)
 
+    place_copies, index_copies, mix_copies = [], [], []
+    half_copies = [[] for _ in range(chunks)]
+
+    def send_half(c, piece, begin, end):
+        for d in range(1, lam_n):
+            peer = lax.rem(lam_me + d, lam_n)
+            copy = pltpu.make_async_remote_copy(
+                src_ref=half_send.at[peer, c, pl.ds(begin, end - begin)],
+                dst_ref=half_held.at[c, lam_me, pl.ds(begin, end - begin)],
+                send_sem=half_ssem.at[c, piece, d], recv_sem=half_rsem.at[c, piece, d],
+                device_id={"lam": peer}, device_id_type=MESH,
+            )
+            copy.start()
+            half_copies[c].append(copy)
+
+    early = groups // 2 * ROW_TILE
     for q in range(groups):
         tile_copies[q].wait()
         part = jnp.dot(
@@ -120,11 +136,10 @@
             half_send[g // chunks, g % chunks, q * ROW_TILE:(q + 1) * ROW_TILE, :] = part[
                 g * ROW_TILE:(g + 1) * ROW_TILE
             ]
-
-    pl.semaphore_wait(barrier, lam_n + pair_n - 2)
-
-    sends = []
-    place_copies, index_copies, half_copies, mix_copies = [], [], [], []
+        if (q + 1) * ROW_TILE == early:
+            pl.semaphore_wait(barrier, lam_n + pair_n - 2)
+            send_half(0, 0, 0, early)
+
     for d in range(1, lam_n):
         peer = lax.rem(lam_me + d, lam_n)
         copy = pltpu.make_async_remote_copy(
@@ -143,19 +158,7 @@
         )
         copy.start()
         index_copies.append(copy)
-    for c in range(chunks):
-        row_copies = []
-        for d in range(1, lam_n):
-            peer = lax.rem(lam_me + d, lam_n)
-            copy = pltpu.make_async_remote_copy(
-                src_ref=half_send.at[peer, c], dst_ref=half_held.at[c, lam_me],
-                send_sem=half_ssem.at[c, d], recv_sem=half_rsem.at[c, d],
-                device_id={"lam": peer}, device_id_type=MESH,
-            )
-            copy.start()
-            row_copies.append(copy)
-        half_copies.append(row_copies)
-
+    send_half(0, 1, early, groups * ROW_TILE)
     place_held[lam_me] = place_ref[...]
     index_held[pair_me] = index_ref[...]
     for c in range(chunks):
@@ -192,6 +195,9 @@
     ]
     for copy in out_copies:
         copy.start()
+
+    for c in range(1, chunks):
+        send_half(c, 0, 0, groups * ROW_TILE)
 
     for copy in place_copies:
         copy.wait_recv()
@@ -352,8 +358,8 @@
             dma((lam_n,)),
             dma((pair_n,)),
             dma((pair_n,)),
-            dma((chunks, lam_n)),
-            dma((chunks, lam_n)),
+            dma((chunks, 2, lam_n)),
+            dma((chunks, 2, lam_n)),
             dma((chunks, pair_n)),
             dma((chunks, pair_n)),
         ],

time: 59.6 us -> 59.1 us (level)
  no operation moved by 1% of the time
where the time goes in v5:
time: 59.1 us; the launch traced here: 58.5 us
  Pallas kernels  57.9 us (98%)
  between operations  0.66 us (1%)
    pallas_call x1, Pallas kernels, on_device(): pl.pallas_call(functools.partial(exchange_kernel, lam_n, pair_n, chunks,...  36.7 us
    pallas_call x1, Pallas kernels, on_device(): pl.pallas_call(functools.partial(product_kernel, share), out_shape=jax.Sh...  21.2 us

profile of v5, /device:TPU:0, one launch (start us, length us, event | category | flops | bytes accessed | tf_op | source)
XLA Modules:
  0.0 58.5 jit_solution(17041892365977509988)
XLA Ops:
  0.7 36.7 %exchange.1 = (bf16[4,160,512]{2,1,0:T(8,128)(2,1)}, bf16[512,2048]{1,0:T(8,128)(2,1)}, bf16[512,1280]{1,0:T(8,128)(2,1)}) custom-call(bf16[2048,1024]{1,0:T(8,128)(2,1)} %bitcast.4, s32[1,8]{1,0:T(1,128)} %pair_hbm.1, s32[1,8]{1,0:T(1,128)} %lam_hbm.1, s32[1,1]{1,0:T(1,128)S(6)} %copy.9.count_hbm, s32[1,64]{1,0:T(1,128)} %bitcast.6, s32[1,64]{1,0:T(1,128)} %bitcast.7, ...), custom_call_target="tpu_custom_call" | custom-call | tf_op jit(solution)/shard_map/exchange/pallas_call | solution.py:322
  37.3 21.2 %product.1 = f32[4,160,20480]{2,1,0:T(8,128)} custom-call(bf16[4,160,512]{2,1,0:T(8,128)(2,1)} %get-tuple-element.8.lhs_ref, bf16[512,2048]{1,0:T(8,128)(2,1)} %get-tuple-element.9.occ_wide_ref, bf16[512,1280]{1,0:T(8,128)(2,1)} %get-tuple-element.10.vir_rows_ref), custom_call_target="tpu_custom_call" | custom-call | tf_op jit(solution)/shard_map/product/pallas_call | solution.py:375
